TPU v7x, 256 devices: a whole 4x4x8 slice. The times are simulated.
256 devices in a mesh: dp: 16 (over y_lo, z), row: 4 (over x), col: 4 (over y_hi, core).
Axes of the slice: x: 4, y: 4 (y_hi: 2, y_lo: 2; y = y_hi * 2 + y_lo), z: 8, core: 2. Of those that a mesh axis runs over, the one named last changes fastest.
Arguments:
- activations: bfloat16 [32768, 2048], P(('dp', 'col'), 'row'), may hold values from -6 to 6
- cotangent: bfloat16 [32768, 16, 512], P(('dp', 'row'), None, 'col'), may hold values from -0.046875 to 0.046875
- weight: bfloat16 [2048, 8192], P('row', ('dp', 'col')), may hold values from -0.046875 to 0.046875
Outputs:
- orthonormal: bfloat16 [2048, 8192], P('row', ('dp', 'col'))
- weight_grad: float32 [2048, 8192], P('row', ('dp', 'col'))
All inputs are finite; a program needn't handle non-finite values.
Results may differ from a plain program's by a relative error of at most 0.0051.
Values may be sent and summed in bfloat16 or wider, within the bound.
A program may use at most 128 MiB of HBM per device.

v0:
```python
import jax
import jax.numpy as jnp
from jax import lax
from jax.sharding import PartitionSpec as P

ITERS = 2


def transpose_product(first_factor, second_factor):
    return lax.dot_general(
        first_factor, second_factor, (((1,), (1,)), ((), ())), preferred_element_type=jnp.float32
    )


def row_panels(local_tile):
    own_rows = lax.all_gather(local_tile, "col", axis=1, tiled=True)
    height = own_rows.shape[0]
    all_rows = lax.all_gather(own_rows, "row", axis=0, tiled=True)
    other_rows = lax.dynamic_slice_in_dim(all_rows, lax.axis_index("col") * height, height, 0)
    return (own_rows, other_rows)


def combine(local_tile, partial_value):
    summed = lax.psum_scatter(partial_value, "col", scatter_dimension=1, tiled=True)
    return 1.5 * local_tile.astype(jnp.float32) - 0.5 * summed


def body(activations, cotangent, weight):
    tokens_all = lax.all_gather(activations, "col", axis=0, tiled=True)
    columns = cotangent.shape[1] * cotangent.shape[2]
    shard_piece = lax.all_gather(cotangent, "row", axis=0, tiled=True)
    flat_piece = shard_piece.reshape(shard_piece.shape[0], columns)
    partial_value = lax.dot_general(
        tokens_all, flat_piece, (((0,), (0,)), ((), ())), preferred_element_type=jnp.float32
    )
    partial_value = partial_value.reshape(
        activations.shape[1], cotangent.shape[1], cotangent.shape[2]
    )
    summed = lax.psum(partial_value, "dp")
    own_block = lax.dynamic_index_in_dim(summed, lax.axis_index("dp"), 1, keepdims=False)
    grad_tile = own_block.astype(jnp.bfloat16)
    iterate = weight
    stored = []
    for counter in range(ITERS):
        own_rows, other_rows = row_panels(iterate)
        gram_block = lax.psum(transpose_product(own_rows, other_rows), "dp").astype(jnp.bfloat16)
        stored.append((own_rows, other_rows, gram_block))
        product = jnp.dot(gram_block, other_rows, preferred_element_type=jnp.float32)
        iterate = combine(iterate, product).astype(jnp.bfloat16)
    upstream = grad_tile
    result = upstream.astype(jnp.float32)
    for counter in reversed(range(ITERS)):
        own_rows, other_rows, gram_block = stored[counter]
        up_own, up_other = row_panels(upstream)
        sym_part = transpose_product(up_own, other_rows) + transpose_product(own_rows, up_other)
        symmetric = lax.psum(sym_part, "dp").astype(jnp.bfloat16)
        partial_value = jnp.dot(gram_block, up_other, preferred_element_type=jnp.float32)
        partial_value = partial_value + jnp.dot(
            symmetric, other_rows, preferred_element_type=jnp.float32
        )
        result = combine(upstream, partial_value)
        upstream = result.astype(jnp.bfloat16)
    return (iterate, result)


def solution(mesh):
    placed = (P(("dp", "col"), "row"), P(("dp", "row"), None, "col"), P("row", ("dp", "col")))
    return jax.shard_map(
        body,
        mesh=mesh,
        in_specs=placed,
        out_specs=(P("row", ("dp", "col")), P("row", ("dp", "col"))),
        check_vma=False,
    )
```

profile of v0, /device:TPU:1, one launch (start us, length us, event | category | flops | bytes accessed | tf_op | source)
XLA Modules:
  0.0 707.4 jit_solution(3056130543442089280)
XLA Ops:
  7.2 12.0 %all_gather.30 = bf16[512,512]{1,0:T(8,128)(2,1)} all-gather(bf16[512,128]{1,0:T(8,128)(2,1)} %param.5), channel_id=1, replica_groups=mesh['dp'=16,'row'=4,'col'=4] {'col'}, dimensions={1}, use_global_device_ids=true | all-gather | bytes 655360 | tf_op jit(solution)/shard_map/all_gather | solution.py:16
  21.1 32.6 %all-gather.9.cloned.1.call-done = bf16[2048,512]{1,0:T(8,128)(2,1)} async-done(((bf16[512,512]{1,0:T(8,128)(2,1)}), bf16[2048,512]{1,0:T(8,128)(2,1)}) %all-gather.9.cloned.1.call-update) | async-done | bytes 2097168 | tf_op jit(solution)/shard_map/all_gather | solution.py:18
  53.7 1.5 convolution_bitcast_fusion.1
  55.2 86.1 %all-gather.15.cloned.1.call-done = bf16[2048,16,128]{2,1,0:T(8,128)(2,1)} async-done(((bf16[512,16,128]{2,1,0:T(8,128)(2,1)}), bf16[2048,16,128]{2,1,0:T(8,128)(2,1)}) %all-gather.15.cloned.1.call-update) | async-done | bytes 8388624 | tf_op jit(solution)/shard_map/all_gather | solution.py:31
  141.3 12.5 %copy.9 = bf16[2048,16,128]{0,2,1:T(8,128)(2,1)} copy(bf16[2048,16,128]{2,1,0:T(8,128)(2,1)} %all-gather.15.cloned.1.call-done) | data formatting | bytes 16777216 | tf_op jit(solution)/shard_map/reshape | solution.py:32
  153.8 20.0 %all-gather.13.cloned.1.call-done = bf16[2048,512]{0,1:T(8,128)(2,1)} async-done(((bf16[512,512]{0,1:T(8,128)(2,1)}), bf16[2048,512]{0,1:T(8,128)(2,1)}) %all-gather.13.cloned.1.call-update) | async-done | bytes 2097168 | tf_op jit(solution)/shard_map/all_gather | solution.py:29
  173.7 8.9 %fusion = f32[512,16,128]{2,0,1:T(8,128)} fusion(bf16[2048,16,128]{0,2,1:T(8,128)(2,1)} %copy.9, bf16[2048,512]{0,1:T(8,128)(2,1)} %all-gather.13.cloned.1.call-done), kind=kOutput, calls=%fused_computation | convolution fusion | flops 4294967296 | bytes 14680064 | tf_op jit(solution)/shard_map/dot_general | solution.py:33
  182.7 119.3 %all-reduce.5 = (bf16[512,512]{0,1:T(8,128)(2,1)S(1)}, bf16[512,16,128]{2,0,1:T(8,128)(2,1)}) all-reduce(f32[512,512]{0,1:T(8,128)S(1)} %convolution_bitcast_fusion.1, f32[512,16,128]{2,0,1:T(8,128)} %fusion), channel_id=1, replica_groups=mesh['dp'=16,'row'=4,'col'=4] {'dp'}, use_global_device_ids=true, to_apply=%region_0.0 | all-reduce | flops 1310720 | bytes 7864320 | tf_op jit(solution)/shard_map/psum | solution.py:46
  302.0 2.7 fusion.25
  304.8 37.5 %reduce-scatter.5.cloned.1.call-done = f32[512,128]{1,0:T(8,128)} async-done(((f32[512,512]{1,0:T(8,128)}), f32[512,128]{1,0:T(8,128)}) %reduce-scatter.5.cloned.1.call-update) | async-done | bytes 262160 | tf_op jit(solution)/shard_map/reduce_scatter | solution.py:24
  343.3 9.3 %all_gather.32 = bf16[512,512]{1,0:T(8,128)(2,1)} all-gather(bf16[512,128]{1,0:T(8,128)(2,1)S(1)} %subtract_convert_fusion.1), channel_id=1, replica_groups=mesh['dp'=16,'row'=4,'col'=4] {'col'}, dimensions={1}, use_global_device_ids=true | all-gather | bytes 655360 | tf_op jit(solution)/shard_map/all_gather | solution.py:16
  353.7 9.3 %all-gather = bf16[512,1,512]{2,0,1:T(8,128)(2,1)} all-gather(bf16[512,1,128]{2,0,1:T(8,128)(2,1)S(1)} %dynamic-slice_convert_fusion), channel_id=2, replica_groups=mesh['dp'=16,'row'=4,'col'=4] {'col'}, dimensions={2}, use_global_device_ids=true | all-gather | bytes 655360 | tf_op jit(solution)/shard_map/all_gather | solution.py:16
  363.0 22.1 %all-gather.11.cloned.1.call-done = bf16[2048,512]{1,0:T(8,128)(2,1)} async-done(((bf16[512,512]{1,0:T(8,128)(2,1)}), bf16[2048,512]{1,0:T(8,128)(2,1)}) %all-gather.11.cloned.1.call-update) | async-done | bytes 2097168 | tf_op jit(solution)/shard_map/all_gather | solution.py:18
  385.1 1.7 fusion.4
  386.7 33.6 %all-gather.19.cloned.1.call-done = bf16[2048,1,512]{2,0,1:T(8,128)(2,1)} async-done(((bf16[512,1,512]{2,0,1:T(8,128)(2,1)}), bf16[2048,1,512]{2,0,1:T(8,128)(2,1)}) %all-gather.19.cloned.1.call-update) | async-done | bytes 2097168 | tf_op jit(solution)/shard_map/all_gather | solution.py:18
  420.3 1.5 convolution_add_fusion.2
  421.9 1.5 fusion.20
  423.4 69.6 %all-reduce.6 = (bf16[512,512]{1,0:T(8,128)(2,1)S(1)}, bf16[512,512]{1,0:T(8,128)(2,1)}) all-reduce(f32[512,512]{1,0:T(8,128)S(1)} %fusion.20, f32[512,512]{1,0:T(8,128)S(1)} %convolution_add_fusion.2), channel_id=1, replica_groups=mesh['dp'=16,'row'=4,'col'=4] {'dp'}, use_global_device_ids=true, to_apply=%region_2.3 | all-reduce | flops 524288 | bytes 3145728 | tf_op jit(solution)/shard_map/psum | solution.py:46
  492.9 1.7 fusion.7
  494.6 2.5 convolution_add_fusion.1
  497.2 44.1 %reduce-scatter.9.cloned.1.call-done = f32[512,128]{1,0:T(8,128)} async-done(((f32[512,512]{1,0:T(8,128)}), f32[512,128]{1,0:T(8,128)}) %reduce-scatter.9.cloned.1.call-update) | async-done | bytes 262160 | tf_op jit(solution)/shard_map/reduce_scatter | solution.py:24
  542.3 9.3 %all_gather.38 = bf16[512,512]{1,0:T(8,128)(2,1)} all-gather(bf16[512,128]{1,0:T(8,128)(2,1)S(1)} %fusion.28), channel_id=1, replica_groups=mesh['dp'=16,'row'=4,'col'=4] {'col'}, dimensions={1}, use_global_device_ids=true | all-gather | bytes 655360 | tf_op jit(solution)/shard_map/all_gather | solution.py:16
  551.7 2.5 fusion.18
  554.3 1.5 fusion.23
  555.8 28.3 %all-gather.17.cloned.1.call-done = bf16[2048,512]{1,0:T(8,128)(2,1)} async-done(((bf16[512,512]{1,0:T(8,128)(2,1)}), bf16[2048,512]{1,0:T(8,128)(2,1)}) %all-gather.17.cloned.1.call-update) | async-done | bytes 2097168 | tf_op jit(solution)/shard_map/all_gather | solution.py:18
  584.1 1.6 fusion.3
  585.7 1.5 fusion.14
  587.2 63.3 %all-reduce.7 = bf16[512,512]{1,0:T(8,128)(2,1)S(1)} all-reduce(f32[512,512]{1,0:T(8,128)S(1)} %fusion.3), channel_id=1, replica_groups=mesh['dp'=16,'row'=4,'col'=4] {'dp'}, use_global_device_ids=true, to_apply=%region_7.8 | all-reduce | flops 262144 | bytes 1572864 | tf_op jit(solution)/shard_map/psum | solution.py:56
  650.5 2.5 convolution_add_fusion
  653.0 1.7 subtract_convert_fusion
  654.7 44.2 %reduce-scatter.11.cloned.1.call-done = f32[512,128]{1,0:T(8,128)} async-done(((f32[512,512]{1,0:T(8,128)}), f32[512,128]{1,0:T(8,128)}) %reduce-scatter.11.cloned.1.call-update) | async-done | bytes 262160 | tf_op jit(solution)/shard_map/reduce_scatter | solution.py:24
  698.8 1.7 multiply_subtract_fusion
  (45 shorter events, 5.3 us)
Async XLA Ops:
  7.2 12.8 %copy-start.7 = (bf16[512,512]{1,0:T(8,128)(2,1)S(1)}, bf16[512,512]{1,0:T(8,128)(2,1)}, u32[]{:S(2)}) copy-start(bf16[512,512]{1,0:T(8,128)(2,1)} %param.3) | copy-start | bytes 1572868
  7.2 46.5 %all-gather.9.cloned.1.call-start = ((), (), s32[]{:S(2)}) async-start(), calls=%async_computation.4 | async-start | bytes 2621440 | tf_op jit(solution)/shard_map/all_gather | solution.py:18
  19.2 34.5 %copy-start = (bf16[512,512]{1,0:T(8,128)(2,1)S(1)}, bf16[512,512]{1,0:T(8,128)(2,1)}, u32[]{:S(2)}) copy-start(bf16[512,512]{1,0:T(8,128)(2,1)} %all_gather.30) | copy-start | bytes 1572868
  19.2 122.1 %all-gather.15.cloned.1.call-start = ((), (), s32[]{:S(2)}) async-start(), calls=%async_computation.9 | async-start | bytes 10485760 | tf_op jit(solution)/shard_map/all_gather | solution.py:31
  20.0 153.8 %all-gather.13.cloned.1.call-start = ((), (), s32[]{:S(2)}) async-start(), calls=%async_computation.8 | async-start | bytes 2621440 | tf_op jit(solution)/shard_map/all_gather | solution.py:29
  21.1 321.3 %reduce-scatter.5.cloned.1.call-start = ((), (), s32[]{:S(2)}) async-start(), calls=%async_computation.5 | async-start | bytes 1310720 | tf_op jit(solution)/shard_map/reduce_scatter | solution.py:24
  302.0 50.6 %copy-start.3 = (bf16[512,512]{0,1:T(8,128)(2,1)}, bf16[512,512]{0,1:T(8,128)(2,1)S(1)}, u32[]{:S(2)}) copy-start(bf16[512,512]{0,1:T(8,128)(2,1)S(1)} %get-tuple-element.4) | copy-start | bytes 1572868
  302.0 40.3 %copy-start.8 = (bf16[512,128]{1,0:T(8,128)(2,1)S(1)}, bf16[512,128]{1,0:T(8,128)(2,1)}, u32[]{:S(2)}) copy-start(bf16[512,128]{1,0:T(8,128)(2,1)} %param.5) | copy-start | bytes 393220
  304.7 80.4 %all-gather.11.cloned.1.call-start = ((), (), s32[]{:S(2)}) async-start(), calls=%async_computation.6 | async-start | bytes 2621440 | tf_op jit(solution)/shard_map/all_gather | solution.py:18
  352.6 67.7 %copy-start.1 = (bf16[512,512]{1,0:T(8,128)(2,1)S(1)}, bf16[512,512]{1,0:T(8,128)(2,1)}, u32[]{:S(2)}) copy-start(bf16[512,512]{1,0:T(8,128)(2,1)} %all_gather.32) | copy-start | bytes 1572868
  352.6 67.7 %all-gather.19.cloned.1.call-start = ((), (), s32[]{:S(2)}) async-start(), calls=%async_computation.13 | async-start | bytes 2621440 | tf_op jit(solution)/shard_map/all_gather | solution.py:18
  362.9 178.4 %reduce-scatter.9.cloned.1.call-start = ((), (), s32[]{:S(2)}) async-start(), calls=%async_computation.10 | async-start | bytes 1310720 | tf_op jit(solution)/shard_map/reduce_scatter | solution.py:24
  492.9 4.2 copy-start.5
  492.9 1.7 copy-start.9
  497.1 54.6 %copy-start.6 = (bf16[512,512]{1,0:T(8,128)(2,1)S(1)}, bf16[512,512]{1,0:T(8,128)(2,1)}, u32[]{:S(2)}) copy-start(bf16[512,512]{1,0:T(8,128)(2,1)} %copy-done.5) | copy-start | bytes 1572868
  497.1 87.0 %all-gather.17.cloned.1.call-start = ((), (), s32[]{:S(2)}) async-start(), calls=%async_computation.11 | async-start | bytes 2621440 | tf_op jit(solution)/shard_map/all_gather | solution.py:18
  551.6 2.7 copy-start.2
  551.7 101.4 %reduce-scatter.7.cloned.1.call-start = ((), (), s32[]{:S(2)}) async-start(), calls=%async_computation.7 | async-start | bytes 1310720 | tf_op jit(solution)/shard_map/reduce_scatter | solution.py:24
  554.3 144.6 %reduce-scatter.11.cloned.1.call-start = ((), (), s32[]{:S(2)}) async-start(), calls=%async_computation.12 | async-start | bytes 1310720 | tf_op jit(solution)/shard_map/reduce_scatter | solution.py:24
  584.1 1.6 copy-start.4
Sparse Core Ops, SparseCore 0:
  19.3 34.3 all-gather.8
  55.5 85.7 all-gather.14
  143.1 30.5 all-gather.12
  304.8 37.4 reduce-scatter.4
  352.8 32.2 all-gather.10
  386.9 33.4 all-gather.18
  497.3 44.0 reduce-scatter.8
  551.8 32.2 all-gather.16
  586.9 40.5 reduce-scatter.6
  653.1 45.6 reduce-scatter.10
where the time goes:
time: 708 us; the launch traced here: 707 us
  waiting for transfers between devices  349 us (49%)
  blocking collectives  292 us (41%)
  matrix products  31.5 us (4%)
  local copies, waits for them, and re-layouts  14.5 us (2%)
  between operations  14.3 us (2%)
    psum x2, blocking collectives, body(): lax.psum(transpose_product(own_rows, other_rows), 'dp').astype(jnp.bfloat16)  189 us
    reduce_scatter x4, waiting for transfers between devices, combine(): lax.psum_scatter(partial_value, 'col', scatter_dimension=1, tiled=True)  126 us
    all_gather x4, waiting for transfers between devices, row_panels(): all_rows = lax.all_gather(own_rows, 'row', axis=0, tiled=True)  117 us
    all_gather x1, waiting for transfers between devices, body(): shard_piece = lax.all_gather(cotangent, 'row', axis=0, tiled=True)  86.1 us
    psum x1, blocking collectives, body(): symmetric = lax.psum(sym_part, 'dp').astype(jnp.bfloat16)  63.3 us
    all_gather x4, blocking collectives, row_panels(): own_rows = lax.all_gather(local_tile, 'col', axis=1, tiled=True)  39.8 us
    all_gather x1, waiting for transfers between devices, body(): tokens_all = lax.all_gather(activations, 'col', axis=0, tiled=True)  20 us
  transfers between devices with their start and end apart: 10, of which 9 were waited for; matrix products, arithmetic and copies ran while one was open for 4% of the time, Pallas kernels for 0%

commit v1 on v0

v1 whole, which is shorter than its diff:
```python
import jax
import jax.numpy as jnp
from jax import lax
from jax.experimental import pallas as pl
from jax.experimental.pallas import tpu as pltpu
from jax.sharding import PartitionSpec as P

LOOKAHEAD = 4
PLACES = {
    "sym0": 3, "scatter0": 4, "gather0": 6, "swap0": 8, "product0": 9, "tile0": 11,
    "sym1": 14, "scatter1": 15, "gather1": 17, "swap1": 17,
}


def nt(first, second):
    return lax.dot_general(first, second, (((1,), (1,)), ((), ())), preferred_element_type=jnp.float32)


def nn(first, second):
    return jnp.dot(first, second, preferred_element_type=jnp.float32)


def kernel(
    a_ref, c_ref, w_ref, x_out, g_out,
    a_all, a_t, c_all, own_part, part_send, part_recv,
    own, other, half, cs_send, cs_recv, zs_send, zs_recv, gram, own_prod, ps_send, ps_recv,
    local_sem, a_ss, a_rs, c_ss, c_rs, p_ss, p_rs,
    o_ss, o_rs, q_ss, q_rs, cs_ss, cs_rs, zs_ss, zs_rs, ag_ss, ag_rs, fw_ss, fw_rs, ps_ss, ps_rs,
):
    d, x, c = lax.axis_index("dp"), lax.axis_index("row"), lax.axis_index("col")
    y_lo, z, y_hi, core = d // 8, d % 8, c // 2, c % 2
    y = y_hi * 2 + y_lo

    def dev(x2, y2, z2, core2):
        return ((y2 % 2) * 8 + z2, x2, (y2 // 2) * 2 + core2)

    left, right = dev((x + 3) % 4, y, z, core), dev((x + 1) % 4, y, z, core)
    sibling = dev(x, y, z, 1 - core)
    hops_y = [dev(x, (y + k) % 4, z, core) for k in range(1, 4)]
    hops_z = [dev(x, y, (z + k) % 8, core) for k in range(1, 8)]

    barrier = pltpu.get_barrier_semaphore()
    for target in [left, right, sibling] + hops_y:
        pl.semaphore_signal(barrier, inc=1, device_id=target)

    @pl.loop(1, 16)
    def _(k):
        pl.semaphore_signal(barrier, inc=1, device_id=((d + k) % 16, x, c))

    @pl.when(x != y)
    def _():
        for k in range(4):
            pl.semaphore_signal(barrier, inc=1, device_id=dev(y, k, z, core))

    def remote(src, dst, ss, rs, target):
        return pltpu.make_async_remote_copy(
            src_ref=src, dst_ref=dst, send_sem=ss, recv_sem=rs, device_id=target
        )

    c_rows = pl.ds(pl.multiple_of(x * 512, 512), 512)
    copy_c = pltpu.make_async_copy(c_ref, c_all.at[:, c_rows, :], local_sem.at[0])
    copy_c.start()
    my_cols = pl.ds(pl.multiple_of(y * 128, 128), 128)
    own[0, :, my_cols] = w_ref[...]
    pl.semaphore_wait(barrier, 24)

    def col_of(k):
        return pl.ds(pl.multiple_of(k * 128, 128), 128)

    def own_copy(k, hop):
        return remote(
            own.at[k, :, my_cols], own.at[k, :, my_cols], o_ss.at[k, hop], o_rs.at[k, y],
            dev(x, (y + hop) % 4, z, core),
        )

    def other_copy(k, hop):
        return remote(
            own.at[k, :, my_cols], other.at[k, :, my_cols], q_ss.at[k, hop], q_rs.at[k, y],
            dev((x + hop) % 4, x, z, core),
        )

    def send_tile(k):
        for hop in (2, 1, 3):
            other_copy(k, hop).start()
            own_copy(k, hop).start()

    def wait_tile(k):
        for hop in range(1, 4):
            source = (y + hop) % 4
            view = own.at[k, :, col_of(source)]
            remote(view, view, o_ss.at[k, hop], o_rs.at[k, source], sibling).wait_recv()

        @pl.when(x != y)
        def _():
            for source in range(4):
                view = other.at[k, :, col_of(source)]
                remote(view, view, q_ss.at[k, 0], q_rs.at[k, source], sibling).wait_recv()

        @pl.when(x == y)
        def _():
            other[k] = own[k]

    my_half = pl.multiple_of(core * 256, 256)
    its_half = pl.multiple_of((1 - core) * 256, 256)

    def swap_copy(k):
        return remote(cs_send.at[k], cs_recv.at[k], cs_ss.at[k], cs_rs.at[k], sibling)

    def sym(k, pairs):
        wait_tile(k)

        def block(rows):
            total = None
            for first, second in pairs:
                term = nt(own[first, rows, :], other[second])
                total = term if total is None else total + term
            return total

        cs_send[k] = block(pl.ds(its_half, 256)).astype(jnp.bfloat16)
        swap_copy(k).start()
        half[k] = block(pl.ds(my_half, 256))

    def scatter_copy(k, hop):
        target = (z + hop) % 8
        return remote(
            zs_send.at[k, target], zs_recv.at[k, z], zs_ss.at[k, hop], zs_rs.at[k, z],
            dev(x, y, target, core),
        )

    def scatter(k):
        swap_copy(k).wait_recv()
        total = half[k] + cs_recv[k].astype(jnp.float32)
        half[k] = total
        zs_send[k] = total.astype(jnp.bfloat16).reshape(8, 32, 512)
        for hop in (4, 3, 5, 2, 6, 1, 7):
            scatter_copy(k, hop).start()

    def piece_rows(owner):
        return pl.ds(pl.multiple_of(core * 256 + owner * 32, 32), 32)

    def gather_copy(k, hop):
        view = gram.at[k, piece_rows(z), :]
        return remote(view, view, ag_ss.at[k, hop], ag_rs.at[k, z], dev(x, y, (z + hop) % 8, core))

    def gather(k):
        total = half[k, pl.ds(pl.multiple_of(z * 32, 32), 32), :]
        for hop in range(1, 8):
            source = (z + hop) % 8
            view = zs_recv.at[k, source]
            remote(view, view, zs_ss.at[k, hop], zs_rs.at[k, source], sibling).wait_recv()
            total = total + zs_recv[k, source].astype(jnp.float32)
        gram[k, piece_rows(z), :] = total.astype(jnp.bfloat16)
        for hop in (4, 3, 5, 2, 6, 1, 7):
            gather_copy(k, hop).start()

    def half_copy(k):
        view = gram.at[k, pl.ds(my_half, 256), :]
        return remote(view, view, fw_ss.at[k], fw_rs.at[k], sibling)

    def swap(k):
        for hop in range(1, 8):
            source = (z + hop) % 8
            view = gram.at[k, piece_rows(source), :]
            remote(view, view, ag_ss.at[k, hop], ag_rs.at[k, source], sibling).wait_recv()
        half_copy(k).start()

    def product_copy(k, hop):
        target = (y + hop) % 4
        return remote(
            ps_send.at[k, target], ps_recv.at[k, y], ps_ss.at[k, hop], ps_rs.at[k, y],
            dev(x, target, z, core),
        )

    def product(k, pairs):
        view = gram.at[k, pl.ds(its_half, 256), :]
        remote(view, view, fw_ss.at[k], fw_rs.at[k], sibling).wait_recv()
        for hop in (2, 1, 3, 0):
            target = (y + hop) % 4
            cols = col_of(target)
            total = None
            for matrix, panel in pairs:
                term = nn(gram[matrix], other[panel, :, cols])
                total = term if total is None else total + term
            if hop:
                ps_send[k, target] = total.astype(jnp.bfloat16)
                product_copy(k, hop).start()
            else:
                own_prod[...] = total

    def result(k, tile):
        total = own_prod[...]
        for hop in range(1, 4):
            source = (y + hop) % 4
            view = ps_recv.at[k, source]
            remote(view, view, ps_ss.at[k, hop], ps_rs.at[k, source], sibling).wait_recv()
            total = total + ps_recv[k, source].astype(jnp.float32)
        return 1.5 * own[tile, :, my_cols].astype(jnp.float32) - 0.5 * total

    def finish_tile(k, tile, following):
        own[following, :, my_cols] = result(k, tile).astype(jnp.bfloat16)
        send_tile(following)

    far = dev(x, (y + 2) % 4, z, core)
    far_c = (c + 2) % 4
    a_far = remote(a_ref, a_all.at[c], a_ss.at[0], a_rs.at[c], far)
    a_sib = remote(a_ref, a_all.at[c], a_ss.at[1], a_rs.at[c], sibling)
    a_fwd = remote(a_all.at[far_c], a_all.at[far_c], a_ss.at[2], a_rs.at[far_c], sibling)
    sib_c = y_hi * 2 + 1 - core
    far_sib_c = (sib_c + 2) % 4

    def a_wait(block):
        view = a_all.at[block]
        remote(view, view, a_ss.at[0], a_rs.at[block], sibling).wait_recv()

    def put_transposed(block, ref):
        cols = pl.ds(pl.multiple_of(block * 512, 512), 512)
        a_t[:, cols] = ref[...].T

    def chunk(i):
        return (d + 1 + i) % 16

    def c_copy(i, way):
        view = c_all.at[chunk(i), c_rows, :]
        return remote(view, view, c_ss.at[i, way], c_rs.at[i, way], left if way else right)

    def rows_of(source):
        return pl.ds(pl.multiple_of(source * 512, 512), 512)

    def c_forward(i, way):
        source = (x + 3) % 4 if way == 0 else (x + 1) % 4
        view = c_all.at[chunk(i), rows_of(source), :]
        return remote(view, view, c_ss.at[i, 2], c_rs.at[i, 2], left if way else right)

    def c_wait(i, slot):
        view = c_all.at[chunk(i), rows_of(0), :]
        remote(view, view, c_ss.at[i, slot], c_rs.at[i, slot], sibling).wait_recv()

    def part_copy(i):
        a = chunk(i)
        return remote(part_send.at[a], part_recv.at[d], p_ss.at[a], p_rs.at[d], (a, x, c))

    send_tile(0)
    a_far.start()
    a_sib.start()
    copy_c.wait()
    for i in range(LOOKAHEAD):
        c_copy(i, 0).start()
        c_copy(i, 1).start()
    put_transposed(c, a_ref)
    a_wait(sib_c)
    put_transposed(sib_c, a_all.at[sib_c])

    stages = {
        "sym0": lambda: sym(0, [(0, 0)]),
        "scatter0": lambda: scatter(0),
        "gather0": lambda: gather(0),
        "swap0": lambda: swap(0),
        "product0": lambda: product(0, [(0, 0)]),
        "tile0": lambda: finish_tile(0, 0, 1),
        "sym1": lambda: sym(1, [(1, 1)]),
        "scatter1": lambda: scatter(1),
        "gather1": lambda: gather(1),
        "swap1": lambda: swap(1),
    }

    @pl.loop(0, 17)
    def _(i):
        @pl.when(i + LOOKAHEAD < 16)
        def _():
            c_copy(i + LOOKAHEAD, 0).start()
            c_copy(i + LOOKAHEAD, 1).start()

        @pl.when(i < 16)
        def _():
            c_wait(i, 0)
            c_wait(i, 1)

            @pl.when(i % 2 == 0)
            def _():
                c_forward(i, 0).start()

            @pl.when(i % 2 == 1)
            def _():
                c_forward(i, 1).start()

        @pl.when(i == 0)
        def _():
            a_wait(far_c)
            a_fwd.start()
            put_transposed(far_c, a_all.at[far_c])
            a_wait(far_sib_c)
            put_transposed(far_sib_c, a_all.at[far_sib_c])

        @pl.when(i > 0)
        def _():
            c_wait(i - 1, 2)
            a = chunk(i - 1)
            block = nn(a_t[...], c_all[a])

            @pl.when(i < 16)
            def _():
                part_send[a] = block.astype(jnp.bfloat16)
                part_copy(i - 1).start()

            @pl.when(i == 16)
            def _():
                own_part[...] = block

        for name, place in PLACES.items():
            if place < 17:
                @pl.when(i == place)
                def _(name=name):
                    stages[name]()

    for name, place in PLACES.items():
        if place >= 17:
            stages[name]()

    own_sum = own_part[...]

    @pl.loop(1, 16)
    def _(k):
        source = (d + k) % 16
        view = part_recv.at[source]
        remote(view, view, p_ss.at[source], p_rs.at[source], sibling).wait_recv()

    @pl.loop(0, 8)
    def _(m):
        rows = pl.ds(pl.multiple_of(m * 64, 64), 64)
        total = own_part[rows, :]
        for k in range(1, 16):
            total = total + part_recv[(d + k) % 16, rows, :].astype(jnp.float32)
        own[2, rows, my_cols] = total.astype(jnp.bfloat16)

    send_tile(2)
    product(1, [(1, 1)])
    x_out[...] = result(1, 1).astype(jnp.bfloat16)

    sym(2, [(2, 1), (1, 2)])
    scatter(2)
    gather(2)
    swap(2)
    product(2, [(1, 2), (2, 1)])
    finish_tile(2, 2, 3)
    sym(3, [(3, 0), (0, 3)])
    scatter(3)
    gather(3)
    swap(3)
    product(3, [(0, 3), (3, 0)])
    g_out[...] = result(3, 3)

    for copy in (a_far, a_sib, a_fwd):
        copy.wait_send()

    @pl.loop(0, 16)
    def _(i):
        c_copy(i, 0).wait_send()
        c_copy(i, 1).wait_send()
        c_forward(i, 0).wait_send()

    @pl.loop(0, 15)
    def _(i):
        part_copy(i).wait_send()

    @pl.loop(0, 4)
    def _(k):
        for hop in range(1, 4):
            own_copy(k, hop).wait_send()
            other_copy(k, hop).wait_send()
            product_copy(k, hop).wait_send()
        for hop in range(1, 8):
            scatter_copy(k, hop).wait_send()
            gather_copy(k, hop).wait_send()
        swap_copy(k).wait_send()
        half_copy(k).wait_send()


def body(activations, cotangent, weight):
    chunks = cotangent.transpose(1, 0, 2)
    bf16, f32 = jnp.bfloat16, jnp.float32
    sems = [
        (1,), (3,), (4,), (16, 3), (16, 3), (16,), (16,),
        (4, 4), (4, 4), (4, 4), (4, 4), (4,), (4,), (4, 8), (4, 8), (4, 8), (4, 8), (4,), (4,), (4, 4), (4, 4),
    ]
    buffers = [
        ((4, 512, 512), bf16), ((512, 2048), bf16), ((16, 2048, 128), bf16), ((512, 128), f32),
        ((16, 512, 128), bf16), ((16, 512, 128), bf16),
        ((4, 512, 512), bf16), ((4, 512, 512), bf16), ((4, 256, 512), f32), ((4, 256, 512), bf16),
        ((4, 256, 512), bf16), ((4, 8, 32, 512), bf16), ((4, 8, 32, 512), bf16), ((4, 512, 512), bf16),
        ((512, 128), f32), ((4, 4, 512, 128), bf16), ((4, 4, 512, 128), bf16),
    ]
    vmem = pl.BlockSpec(memory_space=pltpu.VMEM)
    return pl.pallas_call(
        kernel,
        out_shape=(jax.ShapeDtypeStruct((512, 128), bf16), jax.ShapeDtypeStruct((512, 128), f32)),
        in_specs=[vmem, pl.BlockSpec(memory_space=pl.ANY), vmem],
        out_specs=(vmem, vmem),
        scratch_shapes=[pltpu.VMEM(s, t) for s, t in buffers] + [pltpu.SemaphoreType.DMA(s) for s in sems],
        compiler_params=pltpu.CompilerParams(
            collective_id=0, has_side_effects=True, vmem_limit_bytes=56 * 2**20
        ),
    )(activations, chunks, weight)


def solution(mesh):
    placed = (P(("dp", "col"), "row"), P(("dp", "row"), None, "col"), P("row", ("dp", "col")))
    return jax.shard_map(
        body,
        mesh=mesh,
        in_specs=placed,
        out_specs=(P("row", ("dp", "col")), P("row", ("dp", "col"))),
        check_vma=False,
    )
```

time: 708 us -> 246 us (0.35)
  waiting for transfers between devices: 349 us -> 0 us
  blocking collectives: 292 us -> 0 us
  Pallas kernels: 0 us -> 239 us
  matrix products: 31.5 us -> 0 us
  between operations: 14.3 us -> 0.64 us
  local copies, waits for them, and re-layouts: 14.5 us -> 6.72 us
    psum x3 -> x0, blocking collectives: 252 us -> none  [the longest x2 189 us: body(): lax.psum(transpose_product(own_rows, other_rows), 'dp').astype(jnp.bfloat16)]
    pallas_call x0 -> x1, Pallas kernels: none -> 239 us  [body(): pl.pallas_call(kernel, out_shape=(jax.ShapeDtypeStruct((512, 128), bf16),...]
    all_gather x6 -> x0, waiting for transfers between devices: 223 us -> none  [the longest x4 117 us: row_panels(): all_rows = lax.all_gather(own_rows, 'row', axis=0, tiled=True)]
    reduce_scatter x4 -> x0, waiting for transfers between devices: 126 us -> none  [combine(): lax.psum_scatter(partial_value, 'col', scatter_dimension=1, tiled=True)]
    all_gather x4 -> x0, blocking collectives: 39.8 us -> none  [row_panels(): own_rows = lax.all_gather(local_tile, 'col', axis=1, tiled=True)]
    dot_general x13 -> x0, matrix products: 31.5 us -> none  [the longest x6 9.27 us: transpose_product(): lax.dot_general(first_factor, second_factor, (((1,), (1,)), ((), ())), pr...]
    reshape x1 -> x0, local copies, waits for them, and re-layouts: 12.5 us -> none  [body(): flat_piece = shard_piece.reshape(shard_piece.shape[0], columns)]
  transfers between devices with their start and end apart: 10 -> 0, of which waited for: 9 -> 0; matrix products, arithmetic and copies ran while one was open for 4% -> 0% of each run, Pallas kernels for 0% -> 0%
where the time goes in v1:
time: 246 us
  Pallas kernels  239 us (97%)
  local copies, waits for them, and re-layouts  6.72 us (3%)
    pallas_call x1, Pallas kernels, body(): pl.pallas_call(kernel, out_shape=(jax.ShapeDtypeStruct((512, 128), bf16),...  239 us
    unnamed x3, local copies, waits for them, and re-layouts  6.72 us

profile of v1, /device:TPU:1, one launch (start us, length us, event | category | flops | bytes accessed | tf_op | source)
XLA Modules:
  0.0 246.3 jit_solution(13427100069551192426)
XLA Ops:
  0.6 3.5 %copy.7 = bf16[512,16,128]{2,0,1:T(8,128)(2,1)} copy(bf16[512,16,128]{2,1,0:T(8,128)(2,1)} %param.4) | data formatting | bytes 4194304 | tf_op args[1]
  4.1 238.9 %shard_map.50 = (bf16[512,128]{1,0:T(8,128)(2,1)}, f32[512,128]{1,0:T(8,128)}) custom-call(bf16[512,512]{1,0:T(8,128)(2,1)} %a_ref.1, bf16[16,512,128]{2,1,0:T(8,128)(2,1)} %bitcast.3, bf16[512,128]{1,0:T(8,128)(2,1)} %w_ref.1), custom_call_target="tpu_custom_call" | custom-call | tf_op jit(solution)/shard_map/pallas_call | solution.py:393
  243.0 1.6 copy.10
  244.6 1.7 copy.11

commit v2 on v1

v2 whole, which is shorter than its diff:
```python
import jax
import jax.numpy as jnp
from jax import lax
from jax.experimental import pallas as pl
from jax.experimental.pallas import tpu as pltpu
from jax.sharding import PartitionSpec as P

LOOKAHEAD = 4
PLACES = {"sym0": 4, "scatter0": 6, "gather0": 8, "product0": 10, "tile0": 13, "sym1": 16}


def nt(first, second):
    return lax.dot_general(first, second, (((1,), (1,)), ((), ())), preferred_element_type=jnp.float32)


def nn(first, second):
    return jnp.dot(first, second, preferred_element_type=jnp.float32)


def kernel(
    a_ref, c_ref, w_ref, x_out, g_out,
    a_all, a_t, c_all, own_part, part_send, part_recv,
    own, other, half, cs_send, cs_recv, zs_send, zs_recv, gram, own_prod, ps_send, ps_recv,
    local_sem, a_ss, a_rs, c_ss, c_rs, p_ss, p_rs,
    o_ss, o_rs, q_ss, q_rs, cs_ss, cs_rs, zs_ss, zs_rs, ag_ss, ag_rs, fw_ss, fw_rs, ps_ss, ps_rs,
):
    d, x, c = lax.axis_index("dp"), lax.axis_index("row"), lax.axis_index("col")
    y_lo, z, y_hi, core = d // 8, d % 8, c // 2, c % 2
    y = y_hi * 2 + y_lo

    def dev(x2, y2, z2, core2):
        return ((y2 % 2) * 8 + z2, x2, (y2 // 2) * 2 + core2)

    left, right = dev((x + 3) % 4, y, z, core), dev((x + 1) % 4, y, z, core)
    sibling = dev(x, y, z, 1 - core)
    hops_y = [dev(x, (y + k) % 4, z, core) for k in range(1, 4)]
    hops_z = [dev(x, y, (z + k) % 8, core) for k in range(1, 8)]

    barrier = pltpu.get_barrier_semaphore()
    for target in [left, right, sibling] + hops_y:
        pl.semaphore_signal(barrier, inc=1, device_id=target)

    @pl.loop(1, 16)
    def _(k):
        pl.semaphore_signal(barrier, inc=1, device_id=((d + k) % 16, x, c))

    @pl.when(x != y)
    def _():
        for k in range(4):
            pl.semaphore_signal(barrier, inc=1, device_id=dev(y, k, z, core))

    def remote(src, dst, ss, rs, target):
        return pltpu.make_async_remote_copy(
            src_ref=src, dst_ref=dst, send_sem=ss, recv_sem=rs, device_id=target
        )

    c_rows = pl.ds(pl.multiple_of(x * 512, 512), 512)
    copy_c = pltpu.make_async_copy(c_ref, c_all.at[:, c_rows, :], local_sem.at[0])
    copy_c.start()
    my_cols = pl.ds(pl.multiple_of(y * 128, 128), 128)
    own[0, :, my_cols] = w_ref[...]

    def put_transposed(block, ref):
        cols = pl.ds(pl.multiple_of(block * 512, 512), 512)
        a_t[:, cols] = ref[...].T

    put_transposed(c, a_ref)
    pl.semaphore_wait(barrier, 24)

    def col_of(k):
        return pl.ds(pl.multiple_of(k * 128, 128), 128)

    def chunk_rows(j):
        return pl.ds(j * 256, 256)

    def core_rows(j, h):
        return pl.ds(pl.multiple_of(j * 256 + h * 128, 128), 128)

    def own_copy(k, j, hop):
        view = own.at[k, chunk_rows(j), my_cols]
        return remote(
            view, view, o_ss.at[k, j, hop], o_rs.at[k, j, y], dev(x, (y + hop) % 4, z, core)
        )

    def other_copy(k, j, hop):
        return remote(
            own.at[k, chunk_rows(j), my_cols], other.at[k, chunk_rows(j), my_cols],
            q_ss.at[k, j, hop], q_rs.at[k, j, y], dev((x + hop) % 4, x, z, core),
        )

    def send_tile(k, j):
        for hop in (2, 1, 3):
            other_copy(k, j, hop).start()
            own_copy(k, j, hop).start()

    def wait_own(k, j):
        for hop in range(1, 4):
            source = (y + hop) % 4
            view = own.at[k, chunk_rows(j), col_of(source)]
            remote(view, view, o_ss.at[k, j, hop], o_rs.at[k, j, source], sibling).wait_recv()

    def wait_tile(k):
        for j in range(2):
            wait_own(k, j)

        @pl.when(x != y)
        def _():
            for j in range(2):
                for source in range(4):
                    view = other.at[k, chunk_rows(j), col_of(source)]
                    remote(view, view, q_ss.at[k, j, 0], q_rs.at[k, j, source], sibling).wait_recv()

        @pl.when(x == y)
        def _():
            other[k] = own[k]

    def swap_copy(k, j):
        return remote(cs_send.at[k, j], cs_recv.at[k, j], cs_ss.at[k, j], cs_rs.at[k, j], sibling)

    def sym(k, pairs):
        wait_tile(k)

        def block(rows):
            total = None
            for first, second in pairs:
                term = nt(own[first, rows, :], other[second])
                total = term if total is None else total + term
            return total

        for j in range(2):
            cs_send[k, j] = block(core_rows(j, 1 - core)).astype(jnp.bfloat16)
            swap_copy(k, j).start()
        for j in range(2):
            half[k, j] = block(core_rows(j, core))

    def scatter_copy(k, j, hop):
        target = (z + hop) % 8
        return remote(
            zs_send.at[k, j, target], zs_recv.at[k, j, z], zs_ss.at[k, j, hop], zs_rs.at[k, j, z],
            dev(x, y, target, core),
        )

    def scatter(k):
        for j in range(2):
            swap_copy(k, j).wait_recv()
            total = half[k, j] + cs_recv[k, j].astype(jnp.float32)
            half[k, j] = total
            zs_send[k, j] = total.astype(jnp.bfloat16).reshape(8, 16, 512)
            for hop in (4, 3, 5, 2, 6, 1, 7):
                scatter_copy(k, j, hop).start()

    def piece_rows(j, owner):
        return pl.ds(pl.multiple_of(j * 256 + core * 128 + owner * 16, 16), 16)

    def gather_copy(k, j, hop):
        view = gram.at[k, piece_rows(j, z), :]
        return remote(
            view, view, ag_ss.at[k, j, hop], ag_rs.at[k, j, z], dev(x, y, (z + hop) % 8, core)
        )

    def gather(k):
        for j in range(2):
            total = half[k, j, pl.ds(pl.multiple_of(z * 16, 16), 16), :]
            for hop in range(1, 8):
                source = (z + hop) % 8
                view = zs_recv.at[k, j, source]
                remote(view, view, zs_ss.at[k, j, hop], zs_rs.at[k, j, source], sibling).wait_recv()
                total = total + zs_recv[k, j, source].astype(jnp.float32)
            gram[k, piece_rows(j, z), :] = total.astype(jnp.bfloat16)
            for hop in (4, 3, 5, 2, 6, 1, 7):
                gather_copy(k, j, hop).start()

    def half_copy(k, j):
        view = gram.at[k, core_rows(j, core), :]
        return remote(view, view, fw_ss.at[k, j], fw_rs.at[k, j], sibling)

    def swap(k, j):
        for hop in range(1, 8):
            source = (z + hop) % 8
            view = gram.at[k, piece_rows(j, source), :]
            remote(view, view, ag_ss.at[k, j, hop], ag_rs.at[k, j, source], sibling).wait_recv()
        half_copy(k, j).start()

    def product_copy(k, j, hop):
        target = (y + hop) % 4
        return remote(
            ps_send.at[k, target, chunk_rows(j)], ps_recv.at[k, y, chunk_rows(j)],
            ps_ss.at[k, j, hop], ps_rs.at[k, j, y], dev(x, target, z, core),
        )

    def product(k, j, pairs):
        view = gram.at[k, core_rows(j, 1 - core), :]
        remote(view, view, fw_ss.at[k, j], fw_rs.at[k, j], sibling).wait_recv()
        rows = chunk_rows(j)
        for hop in (2, 1, 3, 0):
            target = (y + hop) % 4
            cols = col_of(target)
            total = None
            for matrix, panel in pairs:
                term = nn(gram[matrix, rows, :], other[panel, :, cols])
                total = term if total is None else total + term
            if hop:
                ps_send[k, target, rows] = total.astype(jnp.bfloat16)
                product_copy(k, j, hop).start()
            else:
                own_prod[rows, :] = total

    def swap_product(k, pairs):
        for j in range(2):
            swap(k, j)
            product(k, j, pairs)

    def result(k, j, tile):
        rows = chunk_rows(j)
        total = own_prod[rows, :]
        for hop in range(1, 4):
            source = (y + hop) % 4
            view = ps_recv.at[k, source, rows]
            remote(view, view, ps_ss.at[k, j, hop], ps_rs.at[k, j, source], sibling).wait_recv()
            total = total + ps_recv[k, source, rows].astype(jnp.float32)
        return 1.5 * own[tile, rows, my_cols].astype(jnp.float32) - 0.5 * total

    def finish_tile(k, tile, following):
        for j in range(2):
            own[following, chunk_rows(j), my_cols] = result(k, j, tile).astype(jnp.bfloat16)
            send_tile(following, j)

    def drain(k):
        for j in range(2):
            for hop in range(1, 4):
                own_copy(k, j, hop).wait_send()
                other_copy(k, j, hop).wait_send()
                product_copy(k, j, hop).wait_send()
            for hop in range(1, 8):
                scatter_copy(k, j, hop).wait_send()
                gather_copy(k, j, hop).wait_send()
            swap_copy(k, j).wait_send()
            half_copy(k, j).wait_send()

    far = dev(x, (y + 2) % 4, z, core)
    far_c = (c + 2) % 4
    a_far = remote(a_ref, a_all.at[c], a_ss.at[0], a_rs.at[c], far)
    a_sib = remote(a_ref, a_all.at[c], a_ss.at[1], a_rs.at[c], sibling)
    a_fwd = remote(a_all.at[far_c], a_all.at[far_c], a_ss.at[2], a_rs.at[far_c], sibling)
    sib_c = y_hi * 2 + 1 - core
    far_sib_c = (sib_c + 2) % 4

    def a_wait(block):
        view = a_all.at[block]
        remote(view, view, a_ss.at[0], a_rs.at[block], sibling).wait_recv()

    def chunk(i):
        return (d + 1 + i) % 16

    def c_copy(i, way):
        view = c_all.at[chunk(i), c_rows, :]
        return remote(view, view, c_ss.at[i, way], c_rs.at[i, way], left if way else right)

    def rows_of(source):
        return pl.ds(pl.multiple_of(source * 512, 512), 512)

    def c_forward(i, way):
        source = (x + 3) % 4 if way == 0 else (x + 1) % 4
        view = c_all.at[chunk(i), rows_of(source), :]
        return remote(view, view, c_ss.at[i, 2], c_rs.at[i, 2], left if way else right)

    def c_wait(i, slot):
        view = c_all.at[chunk(i), rows_of(0), :]
        remote(view, view, c_ss.at[i, slot], c_rs.at[i, slot], sibling).wait_recv()

    def part_copy(i):
        a = chunk(i)
        return remote(part_send.at[a], part_recv.at[d], p_ss.at[a], p_rs.at[d], (a, x, c))

    send_tile(0, 0)
    send_tile(0, 1)
    a_far.start()
    a_sib.start()
    copy_c.wait()
    for i in range(LOOKAHEAD):
        c_copy(i, 0).start()
        c_copy(i, 1).start()
    a_wait(sib_c)
    put_transposed(sib_c, a_all.at[sib_c])

    stages = {
        "sym0": lambda: sym(0, [(0, 0)]),
        "scatter0": lambda: scatter(0),
        "gather0": lambda: gather(0),
        "product0": lambda: swap_product(0, [(0, 0)]),
        "tile0": lambda: finish_tile(0, 0, 1),
        "sym1": lambda: sym(1, [(1, 1)]),
    }

    @pl.loop(0, 17)
    def _(i):
        @pl.when(i + LOOKAHEAD < 16)
        def _():
            c_copy(i + LOOKAHEAD, 0).start()
            c_copy(i + LOOKAHEAD, 1).start()

        @pl.when(i < 16)
        def _():
            c_wait(i, 0)
            c_wait(i, 1)

            @pl.when(i % 2 == 0)
            def _():
                c_forward(i, 0).start()

            @pl.when(i % 2 == 1)
            def _():
                c_forward(i, 1).start()

        @pl.when(i == 0)
        def _():
            a_wait(far_c)
            a_fwd.start()
            put_transposed(far_c, a_all.at[far_c])
            a_wait(far_sib_c)
            put_transposed(far_sib_c, a_all.at[far_sib_c])

        @pl.when(i > 0)
        def _():
            c_wait(i - 1, 2)
            a = chunk(i - 1)
            block = nn(a_t[...], c_all[a])

            @pl.when(i < 16)
            def _():
                part_send[a] = block.astype(jnp.bfloat16)
                part_copy(i - 1).start()

            @pl.when(i == 16)
            def _():
                own_part[...] = block

        for name, place in PLACES.items():
            if place < 17:
                @pl.when(i == place)
                def _(name=name):
                    stages[name]()


    @pl.loop(1, 16)
    def _(k):
        source = (d + k) % 16
        view = part_recv.at[source]
        remote(view, view, p_ss.at[source], p_rs.at[source], sibling).wait_recv()

    @pl.loop(0, 8)
    def _(m):
        rows = pl.ds(pl.multiple_of(m * 64, 64), 64)
        total = own_part[rows, :]
        for k in range(1, 16):
            total = total + part_recv[(d + k) % 16, rows, :].astype(jnp.float32)
        own[2, rows, my_cols] = total.astype(jnp.bfloat16)

    send_tile(2, 0)
    send_tile(2, 1)
    scatter(1)
    for copy in (a_far, a_sib, a_fwd):
        copy.wait_send()

    @pl.loop(0, 16)
    def _(i):
        c_copy(i, 0).wait_send()
        c_copy(i, 1).wait_send()
        c_forward(i, 0).wait_send()

    @pl.loop(0, 15)
    def _(i):
        part_copy(i).wait_send()

    sym(2, [(2, 1), (1, 2)])
    gather(1)
    scatter(2)
    drain(0)
    swap_product(1, [(1, 1)])
    gather(2)
    for j in range(2):
        x_out[chunk_rows(j), :] = result(1, j, 1).astype(jnp.bfloat16)
    drain(1)
    swap_product(2, [(1, 2), (2, 1)])
    finish_tile(2, 2, 3)
    drain(2)
    sym(3, [(3, 0), (0, 3)])
    scatter(3)
    gather(3)
    swap_product(3, [(0, 3), (3, 0)])
    for j in range(2):
        g_out[chunk_rows(j), :] = result(3, j, 3)
    drain(3)


def body(activations, cotangent, weight):
    chunks = cotangent.transpose(1, 0, 2)
    bf16, f32 = jnp.bfloat16, jnp.float32
    sems = [
        (1,), (3,), (4,), (16, 3), (16, 3), (16,), (16,),
        (4, 2, 4), (4, 2, 4), (4, 2, 4), (4, 2, 4), (4, 2), (4, 2), (4, 2, 8), (4, 2, 8), (4, 2, 8), (4, 2, 8),
        (4, 2), (4, 2), (4, 2, 4), (4, 2, 4),
    ]
    buffers = [
        ((4, 512, 512), bf16), ((512, 2048), bf16), ((16, 2048, 128), bf16), ((512, 128), f32),
        ((16, 512, 128), bf16), ((16, 512, 128), bf16),
        ((4, 512, 512), bf16), ((4, 512, 512), bf16), ((4, 2, 128, 512), f32), ((4, 2, 128, 512), bf16),
        ((4, 2, 128, 512), bf16), ((4, 2, 8, 16, 512), bf16), ((4, 2, 8, 16, 512), bf16), ((4, 512, 512), bf16),
        ((512, 128), f32), ((4, 4, 512, 128), bf16), ((4, 4, 512, 128), bf16),
    ]
    vmem = pl.BlockSpec(memory_space=pltpu.VMEM)
    return pl.pallas_call(
        kernel,
        out_shape=(jax.ShapeDtypeStruct((512, 128), bf16), jax.ShapeDtypeStruct((512, 128), f32)),
        in_specs=[vmem, pl.BlockSpec(memory_space=pl.ANY), vmem],
        out_specs=(vmem, vmem),
        scratch_shapes=[pltpu.VMEM(s, t) for s, t in buffers] + [pltpu.SemaphoreType.DMA(s) for s in sems],
        compiler_params=pltpu.CompilerParams(
            collective_id=0, has_side_effects=True, vmem_limit_bytes=56 * 2**20
        ),
    )(activations, chunks, weight)


def solution(mesh):
    placed = (P(("dp", "col"), "row"), P(("dp", "row"), None, "col"), P("row", ("dp", "col")))
    return jax.shard_map(
        body,
        mesh=mesh,
        in_specs=placed,
        out_specs=(P("row", ("dp", "col")), P("row", ("dp", "col"))),
        check_vma=False,
    )
```

time: 246 us -> 218 us (0.89)
  Pallas kernels: 239 us -> 211 us
    pallas_call x1, Pallas kernels: 239 us -> 211 us  [body(): pl.pallas_call(kernel, out_shape=(jax.ShapeDtypeStruct((512, 128), bf16),...]
where the time goes in v2:
time: 218 us
  Pallas kernels  211 us (97%)
  local copies, waits for them, and re-layouts  6.72 us (3%)
    pallas_call x1, Pallas kernels, body(): pl.pallas_call(kernel, out_shape=(jax.ShapeDtypeStruct((512, 128), bf16),...  211 us
    unnamed x3, local copies, waits for them, and re-layouts  6.72 us

profile of v2, /device:TPU:1, one launch (start us, length us, event | category | flops | bytes accessed | tf_op | source)
XLA Modules:
  0.0 218.1 jit_solution(1555896073885046383)
XLA Ops:
  0.6 3.5 %copy.7 = bf16[512,16,128]{2,0,1:T(8,128)(2,1)} copy(bf16[512,16,128]{2,1,0:T(8,128)(2,1)} %param.4) | data formatting | bytes 4194304 | tf_op args[1]
  4.1 210.8 %shard_map.50 = (bf16[512,128]{1,0:T(8,128)(2,1)}, f32[512,128]{1,0:T(8,128)}) custom-call(bf16[512,512]{1,0:T(8,128)(2,1)} %a_ref.1, bf16[16,512,128]{2,1,0:T(8,128)(2,1)} %bitcast.3, bf16[512,128]{1,0:T(8,128)(2,1)} %w_ref.1), custom_call_target="tpu_custom_call" | custom-call | tf_op jit(solution)/shard_map/pallas_call | solution.py:412
  214.9 1.6 copy.10
  216.4 1.7 copy.11

commit v3 on v2

--- a/solution.py
+++ b/solution.py
@@ -6,7 +6,7 @@
 from jax.sharding import PartitionSpec as P
 
 LOOKAHEAD = 4
-PLACES = {"sym0": 4, "scatter0": 6, "gather0": 8, "product0": 10, "tile0": 13, "sym1": 16}
+PLACES = {"sym0": 5, "scatter0": 7, "gather0": 9, "product0": 11, "tile0": 14}
 
 
 def nt(first, second):
@@ -18,7 +18,7 @@
 
 
 def kernel(
-    a_ref, c_ref, w_ref, x_out, g_out,
+    a_ref, c_ref, w_ref, g_out,
     a_all, a_t, c_all, own_part, part_send, part_recv,
     own, other, half, cs_send, cs_recv, zs_send, zs_recv, gram, own_prod, ps_send, ps_recv,
     local_sem, a_ss, a_rs, c_ss, c_rs, p_ss, p_rs,
@@ -203,7 +203,7 @@
                 ps_send[k, target, rows] = total.astype(jnp.bfloat16)
                 product_copy(k, j, hop).start()
             else:
-                own_prod[rows, :] = total
+                own_prod[k, rows, :] = total
 
     def swap_product(k, pairs):
         for j in range(2):
@@ -212,7 +212,7 @@
 
     def result(k, j, tile):
         rows = chunk_rows(j)
-        total = own_prod[rows, :]
+        total = own_prod[k, rows, :]
         for hop in range(1, 4):
             source = (y + hop) % 4
             view = ps_recv.at[k, source, rows]
@@ -250,7 +250,7 @@
         remote(view, view, a_ss.at[0], a_rs.at[block], sibling).wait_recv()
 
     def chunk(i):
-        return (d + 1 + i) % 16
+        return (d + 5 * (i + 1)) % 16
 
     def c_copy(i, way):
         view = c_all.at[chunk(i), c_rows, :]
@@ -348,16 +348,18 @@
         view = part_recv.at[source]
         remote(view, view, p_ss.at[source], p_rs.at[source], sibling).wait_recv()
 
-    @pl.loop(0, 8)
-    def _(m):
-        rows = pl.ds(pl.multiple_of(m * 64, 64), 64)
-        total = own_part[rows, :]
-        for k in range(1, 16):
-            total = total + part_recv[(d + k) % 16, rows, :].astype(jnp.float32)
-        own[2, rows, my_cols] = total.astype(jnp.bfloat16)
-
-    send_tile(2, 0)
-    send_tile(2, 1)
+    for j in range(2):
+        @pl.loop(j * 4, j * 4 + 4)
+        def _(m):
+            rows = pl.ds(pl.multiple_of(m * 64, 64), 64)
+            total = own_part[rows, :]
+            for k in range(1, 16):
+                total = total + part_recv[(d + k) % 16, rows, :].astype(jnp.float32)
+            own[2, rows, my_cols] = total.astype(jnp.bfloat16)
+
+        send_tile(2, j)
+
+    sym(1, [(1, 1)])
     scatter(1)
     for copy in (a_far, a_sib, a_fwd):
         copy.wait_send()
@@ -376,20 +378,23 @@
     gather(1)
     scatter(2)
     drain(0)
-    swap_product(1, [(1, 1)])
+    swap(1, 0)
+    swap(1, 1)
     gather(2)
-    for j in range(2):
-        x_out[chunk_rows(j), :] = result(1, j, 1).astype(jnp.bfloat16)
-    drain(1)
+    product(1, 0, [(1, 1)])
+    product(1, 1, [(1, 1)])
     swap_product(2, [(1, 2), (2, 1)])
     finish_tile(2, 2, 3)
+    for j in range(2):
+        g_out[chunk_rows(j), pl.ds(128, 128)] = result(1, j, 1)
+    drain(1)
     drain(2)
     sym(3, [(3, 0), (0, 3)])
     scatter(3)
     gather(3)
     swap_product(3, [(0, 3), (3, 0)])
     for j in range(2):
-        g_out[chunk_rows(j), :] = result(3, j, 3)
+        g_out[chunk_rows(j), pl.ds(0, 128)] = result(3, j, 3)
     drain(3)
 
 
@@ -406,19 +411,20 @@
         ((16, 512, 128), bf16), ((16, 512, 128), bf16),
         ((4, 512, 512), bf16), ((4, 512, 512), bf16), ((4, 2, 128, 512), f32), ((4, 2, 128, 512), bf16),
         ((4, 2, 128, 512), bf16), ((4, 2, 8, 16, 512), bf16), ((4, 2, 8, 16, 512), bf16), ((4, 512, 512), bf16),
-        ((512, 128), f32), ((4, 4, 512, 128), bf16), ((4, 4, 512, 128), bf16),
+        ((4, 512, 128), f32), ((4, 4, 512, 128), bf16), ((4, 4, 512, 128), bf16),
     ]
     vmem = pl.BlockSpec(memory_space=pltpu.VMEM)
-    return pl.pallas_call(
+    both = pl.pallas_call(
         kernel,
-        out_shape=(jax.ShapeDtypeStruct((512, 128), bf16), jax.ShapeDtypeStruct((512, 128), f32)),
+        out_shape=jax.ShapeDtypeStruct((512, 256), f32),
         in_specs=[vmem, pl.BlockSpec(memory_space=pl.ANY), vmem],
-        out_specs=(vmem, vmem),
+        out_specs=vmem,
         scratch_shapes=[pltpu.VMEM(s, t) for s, t in buffers] + [pltpu.SemaphoreType.DMA(s) for s in sems],
         compiler_params=pltpu.CompilerParams(
             collective_id=0, has_side_effects=True, vmem_limit_bytes=56 * 2**20
         ),
     )(activations, chunks, weight)
+    return both[:, 128:].astype(bf16), both[:, :128]
 
 
 def solution(mesh):

time: 218 us -> 210 us (0.963)
  Pallas kernels: 211 us -> 203 us
    pallas_call x1, Pallas kernels: 211 us -> 203 us  [body(): pl.pallas_call(kernel, out_shape=jax.ShapeDtypeStruct((512, 256), f32), i...]
    slice x0 -> x2, local copies, waits for them, and re-layouts: none -> 3.29 us  [body(): return (both[:, 128:].astype(bf16), both[:, :128])]
    unnamed x3 -> x1, local copies, waits for them, and re-layouts: 6.72 us -> 3.48 us
where the time goes in v3:
time: 210 us
  Pallas kernels  203 us (97%)
  local copies, waits for them, and re-layouts  6.77 us (3%)
    pallas_call x1, Pallas kernels, body(): pl.pallas_call(kernel, out_shape=jax.ShapeDtypeStruct((512, 256), f32), i...  203 us

profile of v3, /device:TPU:1, one launch (start us, length us, event | category | flops | bytes accessed | tf_op | source)
XLA Modules:
  0.0 210.2 jit_solution(2482368339806314781)
XLA Ops:
  0.6 3.5 %copy.7 = bf16[512,16,128]{2,0,1:T(8,128)(2,1)} copy(bf16[512,16,128]{2,1,0:T(8,128)(2,1)} %param.4) | data formatting | bytes 4194304 | tf_op args[1]
  4.1 202.8 %shard_map.50 = f32[512,256]{1,0:T(8,128)} custom-call(bf16[512,512]{1,0:T(8,128)(2,1)} %a_ref.1, bf16[16,512,128]{2,1,0:T(8,128)(2,1)} %bitcast.3, bf16[512,128]{1,0:T(8,128)(2,1)} %w_ref.1), custom_call_target="tpu_custom_call" | custom-call | tf_op jit(solution)/shard_map/pallas_call | solution.py:417
  206.9 1.6 slice.11
  208.5 1.7 slice.8

commit v4 on v3

--- a/solution.py
+++ b/solution.py
@@ -6,7 +6,8 @@
 from jax.sharding import PartitionSpec as P
 
 LOOKAHEAD = 4
-PLACES = {"sym0": 5, "scatter0": 7, "gather0": 9, "product0": 11, "tile0": 14}
+LAG = 4
+PLACES = {"sym0": 6, "scatter0": 8, "gather0": 10, "product0": 12, "tile0": 15}
 
 
 def nt(first, second):
@@ -19,7 +20,7 @@
 
 def kernel(
     a_ref, c_ref, w_ref, g_out,
-    a_all, a_t, c_all, own_part, part_send, part_recv,
+    a_all, a_t, c_all, own_part, part_sum, part_send, part_recv,
     own, other, half, cs_send, cs_recv, zs_send, zs_recv, gram, own_prod, ps_send, ps_recv,
     local_sem, a_ss, a_rs, c_ss, c_rs, p_ss, p_rs,
     o_ss, o_rs, q_ss, q_rs, cs_ss, cs_rs, zs_ss, zs_rs, ag_ss, ag_rs, fw_ss, fw_rs, ps_ss, ps_rs,
@@ -272,12 +273,14 @@
         a = chunk(i)
         return remote(part_send.at[a], part_recv.at[d], p_ss.at[a], p_rs.at[d], (a, x, c))
 
+    copy_c.wait()
+    c_copy(0, 0).start()
+    c_copy(0, 1).start()
     send_tile(0, 0)
     send_tile(0, 1)
     a_far.start()
     a_sib.start()
-    copy_c.wait()
-    for i in range(LOOKAHEAD):
+    for i in range(1, LOOKAHEAD):
         c_copy(i, 0).start()
         c_copy(i, 1).start()
     a_wait(sib_c)
@@ -292,6 +295,16 @@
         "sym1": lambda: sym(1, [(1, 1)]),
     }
 
+    def source_of(k):
+        return (d + 80 - 5 * (k + 1)) % 16
+
+    def part_wait(k):
+        source = source_of(k)
+        view = part_recv.at[source]
+        remote(view, view, p_ss.at[source], p_rs.at[source], sibling).wait_recv()
+
+    part_sum[...] = jnp.zeros_like(part_sum)
+
     @pl.loop(0, 17)
     def _(i):
         @pl.when(i + LOOKAHEAD < 16)
@@ -335,6 +348,11 @@
             def _():
                 own_part[...] = block
 
+        @pl.when(i > LAG)
+        def _():
+            part_wait(i - LAG - 1)
+            part_sum[...] += part_recv[source_of(i - LAG - 1)].astype(jnp.float32)
+
         for name, place in PLACES.items():
             if place < 17:
                 @pl.when(i == place)
@@ -342,19 +360,16 @@
                     stages[name]()
 
 
-    @pl.loop(1, 16)
-    def _(k):
-        source = (d + k) % 16
-        view = part_recv.at[source]
-        remote(view, view, p_ss.at[source], p_rs.at[source], sibling).wait_recv()
+    for k in range(16 - LAG, 15):
+        part_wait(k)
 
     for j in range(2):
         @pl.loop(j * 4, j * 4 + 4)
         def _(m):
             rows = pl.ds(pl.multiple_of(m * 64, 64), 64)
-            total = own_part[rows, :]
-            for k in range(1, 16):
-                total = total + part_recv[(d + k) % 16, rows, :].astype(jnp.float32)
+            total = own_part[rows, :] + part_sum[rows, :]
+            for k in range(16 - LAG, 15):
+                total = total + part_recv[source_of(k), rows, :].astype(jnp.float32)
             own[2, rows, my_cols] = total.astype(jnp.bfloat16)
 
         send_tile(2, j)
@@ -407,7 +422,7 @@
         (4, 2), (4, 2), (4, 2, 4), (4, 2, 4),
     ]
     buffers = [
-        ((4, 512, 512), bf16), ((512, 2048), bf16), ((16, 2048, 128), bf16), ((512, 128), f32),
+        ((4, 512, 512), bf16), ((512, 2048), bf16), ((16, 2048, 128), bf16), ((512, 128), f32), ((512, 128), f32),
         ((16, 512, 128), bf16), ((16, 512, 128), bf16),
         ((4, 512, 512), bf16), ((4, 512, 512), bf16), ((4, 2, 128, 512), f32), ((4, 2, 128, 512), bf16),
         ((4, 2, 128, 512), bf16), ((4, 2, 8, 16, 512), bf16), ((4, 2, 8, 16, 512), bf16), ((4, 512, 512), bf16),

time: 210 us -> 210 us (level)
  no operation moved by 1% of the time
where the time goes in v4:
time: 210 us
  Pallas kernels  202 us (96%)
  local copies, waits for them, and re-layouts  6.77 us (3%)
    pallas_call x1, Pallas kernels, body(): pl.pallas_call(kernel, out_shape=jax.ShapeDtypeStruct((512, 256), f32), i...  202 us

profile of v4, /device:TPU:1, one launch (start us, length us, event | category | flops | bytes accessed | tf_op | source)
XLA Modules:
  0.0 209.8 jit_solution(11899232267906017792)
XLA Ops:
  0.6 3.5 %copy.7 = bf16[512,16,128]{2,0,1:T(8,128)(2,1)} copy(bf16[512,16,128]{2,1,0:T(8,128)(2,1)} %param.4) | data formatting | bytes 4194304 | tf_op args[1]
  4.1 202.4 %shard_map.50 = f32[512,256]{1,0:T(8,128)} custom-call(bf16[512,512]{1,0:T(8,128)(2,1)} %a_ref.1, bf16[16,512,128]{2,1,0:T(8,128)(2,1)} %bitcast.3, bf16[512,128]{1,0:T(8,128)(2,1)} %w_ref.1), custom_call_target="tpu_custom_call" | custom-call | tf_op jit(solution)/shard_map/pallas_call | solution.py:432
  206.5 1.6 slice.11
  208.1 1.7 slice.8

commit v5 on v3

--- a/solution.py
+++ b/solution.py
@@ -20,7 +20,7 @@
 def kernel(
     a_ref, c_ref, w_ref, g_out,
     a_all, a_t, c_all, own_part, part_send, part_recv,
-    own, other, half, cs_send, cs_recv, zs_send, zs_recv, gram, own_prod, ps_send, ps_recv,
+    own, other, half, cs_send, cs_recv, zs_send, zs_recv, gram, prior, own_prod, ps_send, ps_recv,
     local_sem, a_ss, a_rs, c_ss, c_rs, p_ss, p_rs,
     o_ss, o_rs, q_ss, q_rs, cs_ss, cs_rs, zs_ss, zs_rs, ag_ss, ag_rs, fw_ss, fw_rs, ps_ss, ps_rs,
 ):
@@ -195,7 +195,7 @@
         for hop in (2, 1, 3, 0):
             target = (y + hop) % 4
             cols = col_of(target)
-            total = None
+            total = prior[rows, cols] if k >= 2 else None
             for matrix, panel in pairs:
                 term = nn(gram[matrix, rows, :], other[panel, :, cols])
                 total = term if total is None else total + term
@@ -204,6 +204,10 @@
                 product_copy(k, j, hop).start()
             else:
                 own_prod[k, rows, :] = total
+
+    def prepare(matrix, panel):
+        for j in range(2):
+            prior[chunk_rows(j), :] = nn(gram[matrix, chunk_rows(j), :], other[panel])
 
     def swap_product(k, pairs):
         for j in range(2):
@@ -383,7 +387,8 @@
     gather(2)
     product(1, 0, [(1, 1)])
     product(1, 1, [(1, 1)])
-    swap_product(2, [(1, 2), (2, 1)])
+    prepare(1, 2)
+    swap_product(2, [(2, 1)])
     finish_tile(2, 2, 3)
     for j in range(2):
         g_out[chunk_rows(j), pl.ds(128, 128)] = result(1, j, 1)
@@ -392,7 +397,8 @@
     sym(3, [(3, 0), (0, 3)])
     scatter(3)
     gather(3)
-    swap_product(3, [(0, 3), (3, 0)])
+    prepare(0, 3)
+    swap_product(3, [(3, 0)])
     for j in range(2):
         g_out[chunk_rows(j), pl.ds(0, 128)] = result(3, j, 3)
     drain(3)
@@ -411,7 +417,7 @@
         ((16, 512, 128), bf16), ((16, 512, 128), bf16),
         ((4, 512, 512), bf16), ((4, 512, 512), bf16), ((4, 2, 128, 512), f32), ((4, 2, 128, 512), bf16),
         ((4, 2, 128, 512), bf16), ((4, 2, 8, 16, 512), bf16), ((4, 2, 8, 16, 512), bf16), ((4, 512, 512), bf16),
-        ((4, 512, 128), f32), ((4, 4, 512, 128), bf16), ((4, 4, 512, 128), bf16),
+        ((512, 512), f32), ((4, 512, 128), f32), ((4, 4, 512, 128), bf16), ((4, 4, 512, 128), bf16),
     ]
     vmem = pl.BlockSpec(memory_space=pltpu.VMEM)
     both = pl.pallas_call(

time: 210 us -> 210 us (level)
  no operation moved by 1% of the time
where the time goes in v5:
time: 210 us
  Pallas kernels  202 us (96%)
  local copies, waits for them, and re-layouts  6.77 us (3%)
    pallas_call x1, Pallas kernels, body(): pl.pallas_call(kernel, out_shape=jax.ShapeDtypeStruct((512, 256), f32), i...  202 us

profile of v5, /device:TPU:1, one launch (start us, length us, event | category | flops | bytes accessed | tf_op | source)
XLA Modules:
  0.0 209.7 jit_solution(9256028932612414481)
XLA Ops:
  0.6 3.5 %copy.7 = bf16[512,16,128]{2,0,1:T(8,128)(2,1)} copy(bf16[512,16,128]{2,1,0:T(8,128)(2,1)} %param.4) | data formatting | bytes 4194304 | tf_op args[1]
  4.1 202.3 %shard_map.50 = f32[512,256]{1,0:T(8,128)} custom-call(bf16[512,512]{1,0:T(8,128)(2,1)} %a_ref.1, bf16[16,512,128]{2,1,0:T(8,128)(2,1)} %bitcast.3, bf16[512,128]{1,0:T(8,128)(2,1)} %w_ref.1), custom_call_target="tpu_custom_call" | custom-call | tf_op jit(solution)/shard_map/pallas_call | solution.py:423
  206.4 1.6 slice.11
  208.0 1.7 slice.8

commit v6 on v4

--- a/solution.py
+++ b/solution.py
@@ -21,7 +21,7 @@
 def kernel(
     a_ref, c_ref, w_ref, g_out,
     a_all, a_t, c_all, own_part, part_sum, part_send, part_recv,
-    own, other, half, cs_send, cs_recv, zs_send, zs_recv, gram, own_prod, ps_send, ps_recv,
+    own, other, half, cs_send, cs_recv, zs_send, zs_recv, gram, prior, own_prod, ps_send, ps_recv,
     local_sem, a_ss, a_rs, c_ss, c_rs, p_ss, p_rs,
     o_ss, o_rs, q_ss, q_rs, cs_ss, cs_rs, zs_ss, zs_rs, ag_ss, ag_rs, fw_ss, fw_rs, ps_ss, ps_rs,
 ):
@@ -196,7 +196,7 @@
         for hop in (2, 1, 3, 0):
             target = (y + hop) % 4
             cols = col_of(target)
-            total = None
+            total = prior[rows, cols] if k >= 2 else None
             for matrix, panel in pairs:
                 term = nn(gram[matrix, rows, :], other[panel, :, cols])
                 total = term if total is None else total + term
@@ -205,6 +205,10 @@
                 product_copy(k, j, hop).start()
             else:
                 own_prod[k, rows, :] = total
+
+    def prepare(matrix, panel):
+        for j in range(2):
+            prior[chunk_rows(j), :] = nn(gram[matrix, chunk_rows(j), :], other[panel])
 
     def swap_product(k, pairs):
         for j in range(2):
@@ -398,7 +402,8 @@
     gather(2)
     product(1, 0, [(1, 1)])
     product(1, 1, [(1, 1)])
-    swap_product(2, [(1, 2), (2, 1)])
+    prepare(1, 2)
+    swap_product(2, [(2, 1)])
     finish_tile(2, 2, 3)
     for j in range(2):
         g_out[chunk_rows(j), pl.ds(128, 128)] = result(1, j, 1)
@@ -407,7 +412,8 @@
     sym(3, [(3, 0), (0, 3)])
     scatter(3)
     gather(3)
-    swap_product(3, [(0, 3), (3, 0)])
+    prepare(0, 3)
+    swap_product(3, [(3, 0)])
     for j in range(2):
         g_out[chunk_rows(j), pl.ds(0, 128)] = result(3, j, 3)
     drain(3)
@@ -426,7 +432,7 @@
         ((16, 512, 128), bf16), ((16, 512, 128), bf16),
         ((4, 512, 512), bf16), ((4, 512, 512), bf16), ((4, 2, 128, 512), f32), ((4, 2, 128, 512), bf16),
         ((4, 2, 128, 512), bf16), ((4, 2, 8, 16, 512), bf16), ((4, 2, 8, 16, 512), bf16), ((4, 512, 512), bf16),
-        ((4, 512, 128), f32), ((4, 4, 512, 128), bf16), ((4, 4, 512, 128), bf16),
+        ((512, 512), f32), ((4, 512, 128), f32), ((4, 4, 512, 128), bf16), ((4, 4, 512, 128), bf16),
     ]
     vmem = pl.BlockSpec(memory_space=pltpu.VMEM)
     both = pl.pallas_call(

time: 210 us -> 210 us (level)
  no operation moved by 1% of the time
where the time goes in v6:
time: 210 us
  Pallas kernels  202 us (96%)
  local copies, waits for them, and re-layouts  6.77 us (3%)
    pallas_call x1, Pallas kernels, body(): pl.pallas_call(kernel, out_shape=jax.ShapeDtypeStruct((512, 256), f32), i...  202 us

profile of v6, /device:TPU:1, one launch (start us, length us, event | category | flops | bytes accessed | tf_op | source)
XLA Modules:
  0.0 209.8 jit_solution(13313907583650311518)
XLA Ops:
  0.6 3.5 %copy.7 = bf16[512,16,128]{2,0,1:T(8,128)(2,1)} copy(bf16[512,16,128]{2,1,0:T(8,128)(2,1)} %param.4) | data formatting | bytes 4194304 | tf_op args[1]
  4.1 202.4 %shard_map.50 = f32[512,256]{1,0:T(8,128)} custom-call(bf16[512,512]{1,0:T(8,128)(2,1)} %a_ref.1, bf16[16,512,128]{2,1,0:T(8,128)(2,1)} %bitcast.3, bf16[512,128]{1,0:T(8,128)(2,1)} %w_ref.1), custom_call_target="tpu_custom_call" | custom-call | tf_op jit(solution)/shard_map/pallas_call | solution.py:438
  206.5 1.6 slice.11
  208.2 1.7 slice.8
